TPU v7x, 32 devices: a whole 2x2x4 slice. The times are simulated.
32 devices in a mesh: wide: 16 (over z, y, core), narrow: 2 (over x).
Axes of the slice: x: 2, y: 2, z: 4, core: 2. Of those that a mesh axis runs over, the one named last changes fastest.
Arguments:
- initial_warmth_state: float32 [128, 128, 256], P(None, 'wide', 'narrow'), may hold values from -1.5 to 1.5
- diffusivity_coefficient: float32 [128, 128, 256], P(None, 'wide', 'narrow'), may hold values from 0.5 to 8
- heating_supply: float32 [128, 128, 256], P(None, 'wide', 'narrow'), may hold values from -6 to 6
- known_forcing_vector: float32 [128, 128, 256], P(None, 'wide', 'narrow'), as said below
Outputs:
- advanced_warmth_state: float32 [128, 128, 256], P(None, 'wide', 'narrow')
- upcoming_forcing_vector: float32 [128, 128, 256], P(None, 'wide', 'narrow')
Inputs may be any that keep to these rules, and one draw needn't show every extreme that they name: `known_forcing_vector`: values lie within -6 to 6.
All inputs are finite; a program needn't handle non-finite values.
Results may differ from a plain program's by a relative error of at most 0.00035.
Values sent between devices are 32-bit elements; how exact they have to be, the bound alone decides.
A program may use at most 64 MiB of HBM per device.

v0:
```python
import jax
import jax.numpy as jnp
from jax import lax
from jax.sharding import PartitionSpec as P

HALF = 256


def extended(cells, sides, width):
    for axis, dim in sides:
        count = lax.axis_size(axis)
        ends = count - 1
        head = lax.slice_in_dim(cells, 0, width, axis=dim)
        tail = lax.slice_in_dim(cells, cells.shape[dim] - width, cells.shape[dim], axis=dim)
        cells = jnp.concatenate(
            [
                lax.ppermute(tail, axis, [(i, (i + 1) % count) for i in range(ends)]),
                cells,
                lax.ppermute(head, axis, [((i + 1) % count, i) for i in range(ends)]),
            ],
            axis=dim,
        )
    return cells


def solve_lines(below_band, main_band, above_band, right_side):
    length = right_side.shape[0]
    if length == 1:
        return right_side / main_band
    blank = jnp.zeros_like(right_side[:1])
    even_below = below_band[0::2]
    even_main = main_band[0::2]
    even_above = above_band[0::2]
    even_right = right_side[0::2]
    next_below = jnp.concatenate([even_below[1:], blank])
    next_main = jnp.concatenate([even_main[1:], blank + 1.0])
    next_above = jnp.concatenate([even_above[1:], blank])
    next_right = jnp.concatenate([even_right[1:], blank])
    factor_left = -below_band[1::2] / even_main
    factor_right = -above_band[1::2] / next_main
    reduced = solve_lines(
        factor_left * even_below,
        main_band[1::2] + factor_left * even_above + factor_right * next_below,
        factor_right * next_above,
        right_side[1::2] + factor_left * even_right + factor_right * next_right,
    )
    earlier = jnp.concatenate([blank, reduced[:-1]])
    solved_even = (even_right - even_below * earlier - even_above * reduced) / even_main
    return jnp.stack([solved_even, reduced], axis=1).reshape(right_side.shape)


def line_solve(cond, right_side):
    half_ratio = 1.0 * HALF
    blank = jnp.zeros_like(cond[:1])
    padded = jnp.concatenate([blank, cond, blank])
    face_low = 0.5 * (padded[:-2] + padded[1:-1])
    face_high = 0.5 * (padded[1:-1] + padded[2:])
    below_band = jnp.concatenate([blank, -half_ratio * face_low[1:]])
    above_band = jnp.concatenate([-half_ratio * face_high[:-1], blank])
    main_band = 1.0 + half_ratio * (face_low + face_high)
    return solve_lines(below_band, main_band, above_band, right_side)


def operator(padded):
    field = padded[0]
    cond = padded[1]
    centre = field[1:-1, 1:-1, 1:-1]
    middle = cond[1:-1, 1:-1, 1:-1]
    total = 0.5 * (middle + cond[:-2, 1:-1, 1:-1]) * (field[:-2, 1:-1, 1:-1] - centre)
    total = total + 0.5 * (middle + cond[2:, 1:-1, 1:-1]) * (field[2:, 1:-1, 1:-1] - centre)
    total = total + 0.5 * (middle + cond[1:-1, :-2, 1:-1]) * (field[1:-1, :-2, 1:-1] - centre)
    total = total + 0.5 * (middle + cond[1:-1, 2:, 1:-1]) * (field[1:-1, 2:, 1:-1] - centre)
    total = total + 0.5 * (middle + cond[1:-1, 1:-1, :-2]) * (field[1:-1, 1:-1, :-2] - centre)
    total = total + 0.5 * (middle + cond[1:-1, 1:-1, 2:]) * (field[1:-1, 1:-1, 2:] - centre)
    return total


def padded_pair(ghost_padded):
    return jnp.pad(ghost_padded, ((0, 0), (1, 1), (0, 0), (0, 0)))


def solve_second(pieces):
    values, conds = pieces
    return (line_solve(conds, values), conds)


def per_device(initial_warmth_state, diffusivity_coefficient, heating_supply, known_forcing_vector):
    time_ratio = 2.0 * HALF
    first = line_solve(diffusivity_coefficient, time_ratio * known_forcing_vector)
    second, cond_second = solve_second(
        (
            lax.all_to_all(
                jnp.swapaxes(first, 0, 1), "wide", split_axis=1, concat_axis=0, tiled=True
            ),
            lax.all_to_all(
                jnp.swapaxes(diffusivity_coefficient, 0, 1),
                "wide",
                split_axis=1,
                concat_axis=0,
                tiled=True,
            ),
        )
    )
    third_in, cond_third = (
        lax.all_to_all(second, "narrow", split_axis=0, concat_axis=2, tiled=True),
        lax.all_to_all(cond_second, "narrow", split_axis=0, concat_axis=2, tiled=True),
    )
    y_count, x_count, z_count = third_in.shape
    cond_lines = cond_third.reshape(y_count * x_count, z_count).T
    depthwise_pass = line_solve(cond_lines, third_in.reshape(y_count * x_count, z_count).T)
    third_block = depthwise_pass.T.reshape(y_count, x_count, z_count)
    flipped_array = lax.all_to_all(
        lax.all_to_all(third_block, "narrow", split_axis=2, concat_axis=0, tiled=True),
        "wide",
        split_axis=0,
        concat_axis=1,
        tiled=True,
    )
    advanced_warmth_state = initial_warmth_state + jnp.swapaxes(flipped_array, 0, 1)
    ghost_padded = extended(
        jnp.stack([advanced_warmth_state, diffusivity_coefficient]), (("wide", 2), ("narrow", 3)), 1
    )
    upcoming_forcing_vector = heating_supply + operator(padded_pair(ghost_padded))
    return (advanced_warmth_state, upcoming_forcing_vector)


def solution(mesh):
    placed = (
        P(None, "wide", "narrow"),
        P(None, "wide", "narrow"),
        P(None, "wide", "narrow"),
        P(None, "wide", "narrow"),
    )
    return jax.shard_map(
        per_device,
        mesh=mesh,
        in_specs=placed,
        out_specs=(P(None, "wide", "narrow"), P(None, "wide", "narrow")),
        check_vma=False,
    )
```

profile of v0, /device:TPU:13, one launch (start us, length us, event | category | flops | bytes accessed | tf_op | source)
XLA Modules:
  0.0 147.1 jit_solution(10686847486221317631)
XLA Ops:
  0.6 6.7 %all-to-all-start.1 = ((f32[8,128,128]{2,0,1:T(8,128)}), f32[8,128,128]{2,0,1:T(8,128)S(1)}, u32[]{:S(2)}, u32[]{:S(2)}) async-start(f32[8,128,128]{2,0,1:T(8,128)} %bitcast.159), calls=%async_computation.1 | async-start | bytes 1048576 | tf_op jit(solution)/shard_map/all_to_all | solution.py:95
  7.3 1.7 %multiply_add_fusion.2 = (f32[128,8,128]{2,1,0:T(8,128)S(1)}, f32[128,8,128]{2,1,0:T(8,128)S(1)}, f32[128,8,128]{2,1,0:T(8,128)S(1)}) fusion(f32[128,8,128]{2,1,0:T(8,128)} %param.5), kind=kLoop, calls=%fused_computation.71 | loop fusion | flops 917504 | bytes 2097152 | tf_op jit(solution)/shard_map/add | solution.py:60
  12.0 9.0 %all-to-all-done.1 = f32[8,128,128]{2,0,1:T(8,128)S(1)} async-done(((f32[8,128,128]{2,0,1:T(8,128)}), f32[8,128,128]{2,0,1:T(8,128)S(1)}, u32[]{:S(2)}, u32[]{:S(2)}) %all-to-all-start.1) | async-done | bytes 524320 | tf_op jit(solution)/shard_map/all_to_all | solution.py:95
  20.9 5.0 %all-to-all-start = ((f32[8,128,128]{2,0,1:T(8,128)}), f32[8,128,128]{2,0,1:T(8,128)S(1)}, u32[]{:S(2)}, u32[]{:S(2)}) async-start(f32[8,128,128]{2,0,1:T(8,128)} %bitcast.21), calls=%async_computation | async-start | bytes 1048576 | tf_op jit(solution)/shard_map/all_to_all | solution.py:92
  26.8 1.6 %multiply_add_fusion.1 = (f32[128,8,128]{2,1,0:T(8,128)S(1)}, f32[128,8,128]{2,1,0:T(8,128)S(1)}, f32[128,8,128]{2,1,0:T(8,128)S(1)}) fusion(f32[128,8,128]{2,1,0:T(8,128)} %bitcast.29), kind=kLoop, calls=%fused_computation.69 | loop fusion | flops 917504 | bytes 2097152 | tf_op jit(solution)/shard_map/add | solution.py:60
  28.7 10.8 %all-to-all-done = f32[8,128,128]{2,0,1:T(8,128)S(1)} async-done(((f32[8,128,128]{2,0,1:T(8,128)}), f32[8,128,128]{2,0,1:T(8,128)S(1)}, u32[]{:S(2)}, u32[]{:S(2)}) %all-to-all-start) | async-done | bytes 524320 | tf_op jit(solution)/shard_map/all_to_all | solution.py:92
  39.5 3.5 %all-to-all-start.3 = ((f32[128,8,128]{2,1,0:T(8,128)}), f32[128,8,128]{2,1,0:T(8,128)S(1)}, u32[]{:S(2)}, u32[]{:S(2)}) async-start(f32[128,8,128]{2,1,0:T(8,128)} %bitcast.29), calls=%async_computation.3 | async-start | bytes 1048576 | tf_op jit(solution)/shard_map/all_to_all | solution.py:106
  45.7 5.2 %all-to-all-done.3 = f32[128,8,128]{2,1,0:T(8,128)S(1)} async-done(((f32[128,8,128]{2,1,0:T(8,128)}), f32[128,8,128]{2,1,0:T(8,128)S(1)}, u32[]{:S(2)}, u32[]{:S(2)}) %all-to-all-start.3) | async-done | bytes 524320 | tf_op jit(solution)/shard_map/all_to_all | solution.py:106
  50.9 3.5 %all-to-all-start.2 = ((f32[128,8,128]{2,1,0:T(8,128)}), f32[128,8,128]{2,1,0:T(8,128)S(1)}, u32[]{:S(2)}, u32[]{:S(2)}) async-start(f32[128,8,128]{2,1,0:T(8,128)} %bitcast.51), calls=%async_computation.2 | async-start | bytes 1048576 | tf_op jit(solution)/shard_map/all_to_all | solution.py:105
  58.8 2.6 %all-to-all-done.2 = f32[128,8,128]{2,1,0:T(8,128)S(1)} async-done(((f32[128,8,128]{2,1,0:T(8,128)}), f32[128,8,128]{2,1,0:T(8,128)S(1)}, u32[]{:S(2)}, u32[]{:S(2)}) %all-to-all-start.2) | async-done | bytes 524320 | tf_op jit(solution)/shard_map/all_to_all | solution.py:105
  73.2 8.5 %all_to_all.102 = f32[2,1,65536]{2,1,0:T(1,128)S(1)} all-to-all(f32[2,1,65536]{2,1,0:T(1,128)S(1)} %reshape.112), channel_id=1, replica_groups=mesh['wide'=16,'narrow'=2] {'narrow'}, dimensions={0} | all-to-all | bytes 1048576 | tf_op jit(solution)/shard_map/all_to_all | solution.py:113
  82.2 2.3 %reduce = f32[2,65536]{1,0:T(2,128)S(1)} reduce(f32[2,1,65536]{2,1,0:T(1,128)S(1)} %all_to_all.102, f32[]{:T(128)} %broadcast.303), dimensions={1}, to_apply=%all_to_all.88.reduce_sub_computation | reduce | bytes 1048580 | tf_op jit(solution)/shard_map/all_to_all | solution.py:113
  85.7 21.1 %all_to_all.103 = f32[128,8,128]{2,1,0:T(8,128)S(1)} all-to-all(f32[128,8,128]{2,1,0:T(8,128)S(1)} %bitcast.188), channel_id=1, replica_groups=mesh['wide'=16,'narrow'=2] {'wide'}, dimensions={0} | all-to-all | bytes 1048576 | tf_op jit(solution)/shard_map/all_to_all | solution.py:112
  107.4 3.6 %collective-permute-start = (f32[2,128,1,128]{3,2,1,0:T(1,128)S(1)}, f32[2,128,1,128]{3,2,1,0:T(1,128)S(1)}, u32[]{:S(2)}, u32[]{:S(2)}) collective-permute-start(f32[2,128,1,128]{3,2,1,0:T(1,128)S(1)} %get-tuple-element.31), channel_id=1, source_target_pairs={{0,2},{2,4},{4,6},{6,8},{8,10},{10,12},{12,14},{14,16},{16,18},{18... | collective-permute-start | bytes 393224 | tf_op jit(solution)/shard_map/ppermute | solution.py:17
  111.0 1.9 %collective-permute-start.1 = (f32[2,128,1,128]{3,2,1,0:T(1,128)S(1)}, f32[2,128,1,128]{3,2,1,0:T(1,128)S(1)}, u32[]{:S(2)}, u32[]{:S(2)}) collective-permute-start(f32[2,128,1,128]{3,2,1,0:T(1,128)S(1)} %get-tuple-element.32), channel_id=1, source_target_pairs={{2,0},{4,2},{6,4},{8,6},{10,8},{12,10},{14,12},{16,14},{18,16},{20... | collective-permute-start | bytes 393224 | tf_op jit(solution)/shard_map/ppermute | solution.py:19
  113.0 5.2 %collective-permute-done.1 = f32[2,128,1,128]{3,2,1,0:T(1,128)S(1)} collective-permute-done((f32[2,128,1,128]{3,2,1,0:T(1,128)S(1)}, f32[2,128,1,128]{3,2,1,0:T(1,128)S(1)}, u32[]{:S(2)}, u32[]{:S(2)}) %collective-permute-start.1) | collective-permute-done | bytes 131104 | tf_op jit(solution)/shard_map/ppermute | solution.py:19
  118.6 2.0 %fusion.90 = (f32[2,128,10,1]{3,2,1,0:T(8,128)}, f32[2,128,10,1]{3,2,1,0:T(8,128)S(1)}) fusion(f32[2,128,10,128]{3,2,1,0:T(8,128)S(1)} %pad_maximum_fusion), kind=kLoop, calls=%fused_computation.290 | loop fusion | bytes 40960 | tf_op jit(solution)/shard_map/slice | solution.py:14
  120.6 2.2 %copy.453 = f32[2,128,10,1]{1,0,3,2:T(2,128)S(1)} copy(f32[2,128,10,1]{3,2,1,0:T(8,128)} %get-tuple-element.25) | data formatting | bytes 20480 | tf_op jit(solution)/shard_map/slice | solution.py:14
  122.8 2.1 %collective-permute-start.2 = (f32[2,128,10,1]{1,0,3,2:T(2,128)S(1)}, f32[2,128,10,1]{1,0,3,2:T(2,128)S(1)}, u32[]{:S(2)}, u32[]{:S(2)}) collective-permute-start(f32[2,128,10,1]{1,0,3,2:T(2,128)S(1)} %copy.453), channel_id=1, source_target_pairs={{0,1},{2,3},{4,5},{6,7},{8,9},{10,11},{12,13},{14,15},{16,17},{18,... | collective-permute-start | bytes 30728 | tf_op jit(solution)/shard_map/ppermute | solution.py:17
  127.9 2.2 %collective-permute-done.3 = f32[2,128,10,1]{1,0,3,2:T(2,128)S(1)} collective-permute-done((f32[2,128,10,1]{1,0,3,2:T(2,128)S(1)}, f32[2,128,10,1]{1,0,3,2:T(2,128)S(1)}, u32[]{:S(2)}, u32[]{:S(2)}) %collective-permute-start.3) | collective-permute-done | bytes 10272 | tf_op jit(solution)/shard_map/ppermute | solution.py:19
  130.0 2.1 %copy.456 = f32[2,128,10,1]{3,2,1,0:T(8,128)} copy(f32[2,128,10,1]{1,0,3,2:T(2,128)S(1)} %collective-permute-done.3) | data formatting | bytes 20480 | tf_op jit(solution)/shard_map/ppermute | solution.py:19
  132.2 5.2 %select_maximum_fusion = f32[2,130,10,130]{3,2,1,0:T(8,128)S(1)} fusion(f32[2,128,10,1]{3,2,1,0:T(8,128)} %copy.456, f32[2,128,10,1]{3,2,1,0:T(8,128)S(1)} %copy.455, f32[2,128,1,128]{3,2,1,0:T(1,128)S(1)} %collective-permute-done.1, f32[2,128,1,128]{3,2,1,0:T(1,128)S(1)} %collective-permute-done, f32[1,128,8,128]{3,2,1,0:T(8,128)S(1)} %bitcast.162, ...), kind=kLoop, calls=%fused_computation.2 | loop fusion | flops 4732000 | bytes 2683200 | tf_op jit(solution)/shard_map/concatenate | solution.py:15
  137.4 1.8 %slice_bitcast_fusion.1 = (f32[130,10,130]{2,1,0:T(8,128)S(1)}, f32[130,10,130]{2,1,0:T(8,128)}) fusion(f32[2,130,10,130]{3,2,1,0:T(8,128)S(1)} %select_maximum_fusion), kind=kLoop, calls=%fused_computation.9 | loop fusion | bytes 2704000 | tf_op jit(solution)/shard_map/squeeze | solution.py:66
  139.2 7.9 %fusion.15 = f32[128,8,128]{2,1,0:T(8,128)} fusion(f32[128,8,128]{2,1,0:T(8,128)S(1)} %copy-done.6, f32[130,10,130]{2,1,0:T(8,128)} %get-tuple-element.24, f32[130,10,130]{2,1,0:T(8,128)S(1)} %get-tuple-element.23), kind=kLoop, calls=%fused_computation.32 | loop fusion | flops 3932160 | bytes 8388608 | tf_op jit(solution)/shard_map/add | solution.py:123
  (331 shorter events, 26.5 us)
Async XLA Ops:
  0.6 8.4 %copy-start.7 = (f32[128,8,128]{2,1,0:T(8,128)S(1)}, f32[128,8,128]{2,1,0:T(8,128)}, u32[]{:S(2)}) copy-start(f32[128,8,128]{2,1,0:T(8,128)} %param.7) | copy-start | bytes 1572868
  0.6 20.3 %all-to-all-start.1 = ((f32[8,128,128]{2,0,1:T(8,128)}), f32[8,128,128]{2,0,1:T(8,128)S(1)}, u32[]{:S(2)}, u32[]{:S(2)}) async-start(f32[8,128,128]{2,0,1:T(8,128)} %bitcast.159), calls=%async_computation.1 | async-start | bytes 1048576 | tf_op jit(solution)/shard_map/all_to_all | solution.py:95
  20.9 18.6 %all-to-all-start = ((f32[8,128,128]{2,0,1:T(8,128)}), f32[8,128,128]{2,0,1:T(8,128)S(1)}, u32[]{:S(2)}, u32[]{:S(2)}) async-start(f32[8,128,128]{2,0,1:T(8,128)} %bitcast.21), calls=%async_computation | async-start | bytes 1048576 | tf_op jit(solution)/shard_map/all_to_all | solution.py:92
  39.5 11.4 %all-to-all-start.3 = ((f32[128,8,128]{2,1,0:T(8,128)}), f32[128,8,128]{2,1,0:T(8,128)S(1)}, u32[]{:S(2)}, u32[]{:S(2)}) async-start(f32[128,8,128]{2,1,0:T(8,128)} %bitcast.29), calls=%async_computation.3 | async-start | bytes 1048576 | tf_op jit(solution)/shard_map/all_to_all | solution.py:106
  50.9 10.5 %all-to-all-start.2 = ((f32[128,8,128]{2,1,0:T(8,128)}), f32[128,8,128]{2,1,0:T(8,128)S(1)}, u32[]{:S(2)}, u32[]{:S(2)}) async-start(f32[128,8,128]{2,1,0:T(8,128)} %bitcast.51), calls=%async_computation.2 | async-start | bytes 1048576 | tf_op jit(solution)/shard_map/all_to_all | solution.py:105
  61.4 3.8 %copy-start.2 = (f32[128,512]{1,0:T(8,128)S(1)}, f32[128,512]{1,0:T(8,128)}, u32[]{:S(2)}) copy-start(f32[128,512]{1,0:T(8,128)} %slice.1130) | copy-start | bytes 786436
  61.4 3.8 %copy-start.3 = (f32[128,512]{1,0:T(8,128)S(1)}, f32[128,512]{1,0:T(8,128)}, u32[]{:S(2)}) copy-start(f32[128,512]{1,0:T(8,128)} %slice.1119) | copy-start | bytes 786436
  63.4 1.9 %copy-start.4 = (f32[128,512]{1,0:T(8,128)S(1)}, f32[128,512]{1,0:T(8,128)}, u32[]{:S(2)}) copy-start(f32[128,512]{1,0:T(8,128)} %slice.1118) | copy-start | bytes 786436
  85.1 21.7 %copy-start.5 = (f32[128,8,128]{2,1,0:T(8,128)S(1)}, f32[128,8,128]{2,1,0:T(8,128)}, u32[]{:S(2)}) copy-start(f32[128,8,128]{2,1,0:T(8,128)} %param.4) | copy-start | bytes 1572868
  85.6 21.6 %copy-start = (f32[128,8,128]{2,1,0:T(8,128)S(1)}, f32[128,8,128]{2,1,0:T(8,128)}, u32[]{:S(2)}) copy-start(f32[128,8,128]{2,1,0:T(8,128)} %param.5) | copy-start | bytes 1572868
  107.2 25.0 %copy-start.1 = (f32[128,8,128]{2,1,0:T(8,128)}, f32[128,8,128]{2,1,0:T(8,128)S(1)}, u32[]{:S(2)}) copy-start(f32[128,8,128]{2,1,0:T(8,128)S(1)} %bitcast_add_fusion) | copy-start | bytes 1572868
  107.4 5.6 %collective-permute-start = (f32[2,128,1,128]{3,2,1,0:T(1,128)S(1)}, f32[2,128,1,128]{3,2,1,0:T(1,128)S(1)}, u32[]{:S(2)}, u32[]{:S(2)}) collective-permute-start(f32[2,128,1,128]{3,2,1,0:T(1,128)S(1)} %get-tuple-element.31), channel_id=1, source_target_pairs={{0,2},{2,4},{4,6},{6,8},{8,10},{10,12},{12,14},{14,16},{16,18},{18... | collective-permute-start | bytes 393224 | tf_op jit(solution)/shard_map/ppermute | solution.py:17
  111.0 7.2 %collective-permute-start.1 = (f32[2,128,1,128]{3,2,1,0:T(1,128)S(1)}, f32[2,128,1,128]{3,2,1,0:T(1,128)S(1)}, u32[]{:S(2)}, u32[]{:S(2)}) collective-permute-start(f32[2,128,1,128]{3,2,1,0:T(1,128)S(1)} %get-tuple-element.32), channel_id=1, source_target_pairs={{2,0},{4,2},{6,4},{8,6},{10,8},{12,10},{14,12},{16,14},{18,16},{20... | collective-permute-start | bytes 393224 | tf_op jit(solution)/shard_map/ppermute | solution.py:19
  122.8 4.1 %collective-permute-start.2 = (f32[2,128,10,1]{1,0,3,2:T(2,128)S(1)}, f32[2,128,10,1]{1,0,3,2:T(2,128)S(1)}, u32[]{:S(2)}, u32[]{:S(2)}) collective-permute-start(f32[2,128,10,1]{1,0,3,2:T(2,128)S(1)} %copy.453), channel_id=1, source_target_pairs={{0,1},{2,3},{4,5},{6,7},{8,9},{10,11},{12,13},{14,15},{16,17},{18,... | collective-permute-start | bytes 30728 | tf_op jit(solution)/shard_map/ppermute | solution.py:17
  125.6 4.4 %collective-permute-start.3 = (f32[2,128,10,1]{1,0,3,2:T(2,128)S(1)}, f32[2,128,10,1]{1,0,3,2:T(2,128)S(1)}, u32[]{:S(2)}, u32[]{:S(2)}) collective-permute-start(f32[2,128,10,1]{1,0,3,2:T(2,128)S(1)} %copy.454), channel_id=1, source_target_pairs={{1,0},{3,2},{5,4},{7,6},{9,8},{11,10},{13,12},{15,14},{17,16},{19,... | collective-permute-start | bytes 30728 | tf_op jit(solution)/shard_map/ppermute | solution.py:19
  137.4 1.8 %copy-start.6 = (f32[128,8,128]{2,1,0:T(8,128)S(1)}, f32[128,8,128]{2,1,0:T(8,128)}, u32[]{:S(2)}) copy-start(f32[128,8,128]{2,1,0:T(8,128)} %param.6) | copy-start | bytes 1572868
where the time goes:
time: 148 us; the launch traced here: 147 us
  waiting for transfers between devices  35 us (24%)
  blocking collectives  29.6 us (20%)
  local copies, waits for them, and re-layouts  27.9 us (19%)
  starting transfers between devices  27.6 us (19%)
  other arithmetic  24.2 us (16%)
  between operations  2.76 us (2%)
    all_to_all x1, blocking collectives, per_device(): lax.all_to_all(lax.all_to_all(third_block, 'narrow', split_axis=2, concat...  21.1 us
    all_to_all x1, waiting for transfers between devices, per_device(): lax.all_to_all(jnp.swapaxes(first, 0, 1), 'wide', split_axis=1, concat_ax...  10.8 us
    all_to_all x1, waiting for transfers between devices, per_device(): lax.all_to_all(jnp.swapaxes(diffusivity_coefficient, 0, 1), 'wide', split...  8.98 us
    all_to_all x1, blocking collectives, per_device(): lax.all_to_all(third_block, 'narrow', split_axis=2, concat_axis=0, tiled=...  8.48 us
    add x1, other arithmetic, per_device(): heating_supply + operator(padded_pair(ghost_padded))  7.86 us
    ppermute x2, waiting for transfers between devices, extended(): lax.ppermute(head, axis, [((i + 1) % count, i) for i in range(ends)])  7.41 us
    all_to_all x1, starting transfers between devices, per_device(): lax.all_to_all(jnp.swapaxes(diffusivity_coefficient, 0, 1), 'wide', split...  6.7 us
    ppermute x2, starting transfers between devices, extended(): lax.ppermute(tail, axis, [(i, (i + 1) % count) for i in range(ends)])  5.73 us
  transfers between devices with their start and end apart: 8, of which 6 were waited for; matrix products, arithmetic and copies ran while one was open for 10% of the time, Pallas kernels for 0%

commit v1 on v0

--- a/solution.py
+++ b/solution.py
@@ -4,6 +4,29 @@
 from jax.sharding import PartitionSpec as P
 
 HALF = 256
+
+
+def cut_along(array, dim, size):
+    shape = array.shape
+    parts = array.reshape(*shape[:dim], size, shape[dim] // size, *shape[dim + 1 :])
+    return jnp.moveaxis(parts, dim, 0)
+
+
+def laid_out(blocks, dim):
+    blocks = jnp.moveaxis(blocks, 0, dim)
+    dims = blocks.shape
+    return blocks.reshape(*dims[:dim], dims[dim] * dims[dim + 1], *dims[dim + 2 :])
+
+
+def pairwise_exchange(array, axis, split_dim, concat_dim):
+    size, position = (lax.axis_size(axis), lax.axis_index(axis))
+    parts = cut_along(array, split_dim, size)
+    gathered = [parts[position]]
+    for lap in range(1, size):
+        sent = parts[position ^ lap]
+        gathered.append(lax.ppermute(sent, axis, [(i, i ^ lap) for i in range(size)]))
+    parts = jnp.stack(gathered)[position ^ jnp.arange(size)]
+    return laid_out(parts, concat_dim)
 
 
 def extended(cells, sides, width):
@@ -89,9 +112,7 @@
     first = line_solve(diffusivity_coefficient, time_ratio * known_forcing_vector)
     second, cond_second = solve_second(
         (
-            lax.all_to_all(
-                jnp.swapaxes(first, 0, 1), "wide", split_axis=1, concat_axis=0, tiled=True
-            ),
+            pairwise_exchange(jnp.swapaxes(first, 0, 1), "wide", 1, 0),
             lax.all_to_all(
                 jnp.swapaxes(diffusivity_coefficient, 0, 1),
                 "wide",

time: 148 us -> 147 us (level)
  waiting for transfers between devices: 35 us -> 17.7 us
  starting transfers between devices: 27.6 us -> 40.3 us
  blocking collectives: 29.6 us -> 34.7 us
    ppermute x0 -> x15, starting transfers between devices: none -> 17.5 us  [pairwise_exchange(): lax.ppermute(sent, axis, [(i, i ^ lap) for i in range(size)])]
    all_to_all x1 -> x0, waiting for transfers between devices: 10.8 us -> none  [per_device(): lax.all_to_all(jnp.swapaxes(first, 0, 1), 'wide', split_axis=1, concat_ax...]
    all_to_all x1, waiting for transfers between devices: 8.98 us -> 0.01 us  [per_device(): lax.all_to_all(jnp.swapaxes(diffusivity_coefficient, 0, 1), 'wide', split...]
    all_to_all x1, blocking collectives: 21.1 us -> 26.4 us  [per_device(): lax.all_to_all(lax.all_to_all(third_block, 'narrow', split_axis=2, concat...]
    all_to_all x1 -> x0, starting transfers between devices: 4.98 us -> none  [per_device(): lax.all_to_all(jnp.swapaxes(first, 0, 1), 'wide', split_axis=1, concat_ax...]
    ppermute x0 -> x15, waiting for transfers between devices: none -> 3.8 us  [pairwise_exchange(): lax.ppermute(sent, axis, [(i, i ^ lap) for i in range(size)])]
    all_to_all x1, waiting for transfers between devices: 5.18 us -> 2.45 us  [per_device(): lax.all_to_all(cond_second, 'narrow', split_axis=0, concat_axis=2, tiled=...]
    all_to_all x1, waiting for transfers between devices: 2.55 us -> 4.21 us  [per_device(): lax.all_to_all(second, 'narrow', split_axis=0, concat_axis=2, tiled=True)]
  transfers between devices with their start and end apart: 8 -> 22, of which waited for: 6 -> 8; matrix products, arithmetic and copies ran while one was open for 10% -> 8% of each run, Pallas kernels for 0% -> 0%
where the time goes in v1:
time: 147 us; the launch traced here: 146 us
  starting transfers between devices  40.3 us (27%)
  blocking collectives  34.7 us (24%)
  local copies, waits for them, and re-layouts  26.6 us (18%)
  other arithmetic  24.1 us (16%)
  waiting for transfers between devices  17.7 us (12%)
  between operations  3 us (2%)
    all_to_all x1, blocking collectives, per_device(): lax.all_to_all(lax.all_to_all(third_block, 'narrow', split_axis=2, concat...  26.4 us
    ppermute x15, starting transfers between devices, pairwise_exchange(): lax.ppermute(sent, axis, [(i, i ^ lap) for i in range(size)])  17.5 us
    all_to_all x1, blocking collectives, per_device(): lax.all_to_all(third_block, 'narrow', split_axis=2, concat_axis=0, tiled=...  8.27 us
    add x1, other arithmetic, per_device(): heating_supply + operator(padded_pair(ghost_padded))  7.84 us
    ppermute x2, waiting for transfers between devices, extended(): lax.ppermute(head, axis, [((i + 1) % count, i) for i in range(ends)])  7.19 us
    all_to_all x1, starting transfers between devices, per_device(): lax.all_to_all(jnp.swapaxes(diffusivity_coefficient, 0, 1), 'wide', split...  6.7 us
    concatenate x2, other arithmetic, extended(): jnp.concatenate([lax.ppermute(tail, axis, [(i, (i + 1) % count) for i in...  5.6 us
    ppermute x2, starting transfers between devices, extended(): lax.ppermute(tail, axis, [(i, (i + 1) % count) for i in range(ends)])  5.55 us
  transfers between devices with their start and end apart: 22, of which 8 were waited for; matrix products, arithmetic and copies ran while one was open for 8% of the time, Pallas kernels for 0%

profile of v1, /device:TPU:13, one launch (start us, length us, event | category | flops | bytes accessed | tf_op | source)
XLA Modules:
  0.0 146.4 jit_solution(4937889904046270121)
XLA Ops:
  0.6 6.7 %all-to-all-start = ((f32[8,128,128]{2,0,1:T(8,128)}), f32[8,128,128]{2,0,1:T(8,128)S(1)}, u32[]{:S(2)}, u32[]{:S(2)}) async-start(f32[8,128,128]{2,0,1:T(8,128)} %bitcast.239), calls=%async_computation | async-start | bytes 1048576 | tf_op jit(solution)/shard_map/all_to_all | solution.py:116
  15.8 2.6 %collective-permute-start.6 = (f32[8,8,128]{2,1,0:T(8,128)S(1)}, f32[8,8,128]{2,1,0:T(8,128)S(1)}, u32[]{:S(2)}, u32[]{:S(2)}) collective-permute-start(f32[8,8,128]{2,1,0:T(8,128)S(1)} %bitcast.310), channel_id=1, source_target_pairs={{0,14},{2,12},{4,10},{6,8},{8,6},{10,4},{12,2},{14,0},{16,30},{18,... | collective-permute-start | bytes 98312 | tf_op jit(solution)/shard_map/ppermute | solution.py:27
  18.4 2.1 %collective-permute-start.7 = (f32[8,8,128]{2,1,0:T(8,128)S(1)}, f32[8,8,128]{2,1,0:T(8,128)S(1)}, u32[]{:S(2)}, u32[]{:S(2)}) collective-permute-start(f32[8,8,128]{2,1,0:T(8,128)S(1)} %bitcast.307), channel_id=1, source_target_pairs={{0,16},{2,18},{4,20},{6,22},{8,24},{10,26},{12,28},{14,30},{16,0},... | collective-permute-start | bytes 98312 | tf_op jit(solution)/shard_map/ppermute | solution.py:27
  21.0 2.1 %collective-permute-start.9 = (f32[8,8,128]{2,1,0:T(8,128)S(1)}, f32[8,8,128]{2,1,0:T(8,128)S(1)}, u32[]{:S(2)}, u32[]{:S(2)}) collective-permute-start(f32[8,8,128]{2,1,0:T(8,128)S(1)} %bitcast.305), channel_id=1, source_target_pairs={{0,20},{2,22},{4,16},{6,18},{8,28},{10,30},{12,24},{14,26},{16,4},... | collective-permute-start | bytes 98312 | tf_op jit(solution)/shard_map/ppermute | solution.py:27
  31.0 1.8 %collective-permute-done.14 = f32[8,8,128]{2,1,0:T(8,128)S(1)} collective-permute-done((f32[8,8,128]{2,1,0:T(8,128)S(1)}, f32[8,8,128]{2,1,0:T(8,128)S(1)}, u32[]{:S(2)}, u32[]{:S(2)}) %collective-permute-start.14) | collective-permute-done | bytes 32800 | tf_op jit(solution)/shard_map/ppermute | solution.py:27
  34.4 3.5 %all-to-all-start.2 = ((f32[128,8,128]{2,1,0:T(8,128)}), f32[128,8,128]{2,1,0:T(8,128)S(1)}, u32[]{:S(2)}, u32[]{:S(2)}) async-start(f32[128,8,128]{2,1,0:T(8,128)} %bitcast.59), calls=%async_computation.2 | async-start | bytes 1048576 | tf_op jit(solution)/shard_map/all_to_all | solution.py:127
  37.9 1.6 %multiply_add_fusion.1 = (f32[128,8,128]{2,1,0:T(8,128)S(1)}, f32[128,8,128]{2,1,0:T(8,128)S(1)}, f32[128,8,128]{2,1,0:T(8,128)S(1)}) fusion(f32[128,8,128]{2,1,0:T(8,128)} %bitcast.59), kind=kLoop, calls=%fused_computation.70 | loop fusion | flops 917504 | bytes 2097152 | tf_op jit(solution)/shard_map/add | solution.py:83
  43.1 2.4 %all-to-all-done.2 = f32[128,8,128]{2,1,0:T(8,128)S(1)} async-done(((f32[128,8,128]{2,1,0:T(8,128)}), f32[128,8,128]{2,1,0:T(8,128)S(1)}, u32[]{:S(2)}, u32[]{:S(2)}) %all-to-all-start.2) | async-done | bytes 524320 | tf_op jit(solution)/shard_map/all_to_all | solution.py:127
  45.6 3.7 %all-to-all-start.1 = ((f32[128,8,128]{2,1,0:T(8,128)}), f32[128,8,128]{2,1,0:T(8,128)S(1)}, u32[]{:S(2)}, u32[]{:S(2)}) async-start(f32[128,8,128]{2,1,0:T(8,128)} %bitcast.81), calls=%async_computation.1 | async-start | bytes 1048576 | tf_op jit(solution)/shard_map/all_to_all | solution.py:126
  51.6 4.2 %all-to-all-done.1 = f32[128,8,128]{2,1,0:T(8,128)S(1)} async-done(((f32[128,8,128]{2,1,0:T(8,128)}), f32[128,8,128]{2,1,0:T(8,128)S(1)}, u32[]{:S(2)}, u32[]{:S(2)}) %all-to-all-start.1) | async-done | bytes 524320 | tf_op jit(solution)/shard_map/all_to_all | solution.py:126
  67.6 8.3 %all_to_all.84 = f32[2,1,65536]{2,1,0:T(1,128)S(1)} all-to-all(f32[2,1,65536]{2,1,0:T(1,128)S(1)} %reshape.175), channel_id=1, replica_groups=mesh['wide'=16,'narrow'=2] {'narrow'}, dimensions={0} | all-to-all | bytes 1048576 | tf_op jit(solution)/shard_map/all_to_all | solution.py:134
  76.4 2.3 %reduce = f32[2,65536]{1,0:T(2,128)S(1)} reduce(f32[2,1,65536]{2,1,0:T(1,128)S(1)} %all_to_all.84, f32[]{:T(128)} %broadcast.338), dimensions={1}, to_apply=%all_to_all.71.reduce_sub_computation | reduce | bytes 1048580 | tf_op jit(solution)/shard_map/all_to_all | solution.py:134
  79.9 26.4 %all_to_all.85 = f32[128,8,128]{2,1,0:T(8,128)S(1)} all-to-all(f32[128,8,128]{2,1,0:T(8,128)S(1)} %bitcast.268), channel_id=1, replica_groups=mesh['wide'=16,'narrow'=2] {'wide'}, dimensions={0} | all-to-all | bytes 1048576 | tf_op jit(solution)/shard_map/all_to_all | solution.py:133
  106.9 3.6 %collective-permute-start.15 = (f32[2,128,1,128]{3,2,1,0:T(1,128)S(1)}, f32[2,128,1,128]{3,2,1,0:T(1,128)S(1)}, u32[]{:S(2)}, u32[]{:S(2)}) collective-permute-start(f32[2,128,1,128]{3,2,1,0:T(1,128)S(1)} %get-tuple-element.31), channel_id=1, source_target_pairs={{0,2},{2,4},{4,6},{6,8},{8,10},{10,12},{12,14},{14,16},{16,18},{18... | collective-permute-start | bytes 393224 | tf_op jit(solution)/shard_map/ppermute | solution.py:40
  110.5 2.1 %collective-permute-start.16 = (f32[2,128,1,128]{3,2,1,0:T(1,128)S(1)}, f32[2,128,1,128]{3,2,1,0:T(1,128)S(1)}, u32[]{:S(2)}, u32[]{:S(2)}) collective-permute-start(f32[2,128,1,128]{3,2,1,0:T(1,128)S(1)} %get-tuple-element.32), channel_id=1, source_target_pairs={{2,0},{4,2},{6,4},{8,6},{10,8},{12,10},{14,12},{16,14},{18,16},{20... | collective-permute-start | bytes 393224 | tf_op jit(solution)/shard_map/ppermute | solution.py:42
  112.7 5.0 %collective-permute-done.16 = f32[2,128,1,128]{3,2,1,0:T(1,128)S(1)} collective-permute-done((f32[2,128,1,128]{3,2,1,0:T(1,128)S(1)}, f32[2,128,1,128]{3,2,1,0:T(1,128)S(1)}, u32[]{:S(2)}, u32[]{:S(2)}) %collective-permute-start.16) | collective-permute-done | bytes 131104 | tf_op jit(solution)/shard_map/ppermute | solution.py:42
  118.1 2.0 %fusion.91 = (f32[2,128,10,1]{3,2,1,0:T(8,128)}, f32[2,128,10,1]{3,2,1,0:T(8,128)S(1)}) fusion(f32[2,128,10,128]{3,2,1,0:T(8,128)S(1)} %pad_maximum_fusion), kind=kLoop, calls=%fused_computation.342 | loop fusion | bytes 40960 | tf_op jit(solution)/shard_map/slice | solution.py:37
  120.1 2.2 %copy.551 = f32[2,128,10,1]{1,0,3,2:T(2,128)S(1)} copy(f32[2,128,10,1]{3,2,1,0:T(8,128)} %get-tuple-element.25) | data formatting | bytes 20480 | tf_op jit(solution)/shard_map/slice | solution.py:37
  122.3 1.9 %collective-permute-start.17 = (f32[2,128,10,1]{1,0,3,2:T(2,128)S(1)}, f32[2,128,10,1]{1,0,3,2:T(2,128)S(1)}, u32[]{:S(2)}, u32[]{:S(2)}) collective-permute-start(f32[2,128,10,1]{1,0,3,2:T(2,128)S(1)} %copy.551), channel_id=1, source_target_pairs={{0,1},{2,3},{4,5},{6,7},{8,9},{10,11},{12,13},{14,15},{16,17},{18,... | collective-permute-start | bytes 30728 | tf_op jit(solution)/shard_map/ppermute | solution.py:40
  127.2 2.2 %collective-permute-done.18 = f32[2,128,10,1]{1,0,3,2:T(2,128)S(1)} collective-permute-done((f32[2,128,10,1]{1,0,3,2:T(2,128)S(1)}, f32[2,128,10,1]{1,0,3,2:T(2,128)S(1)}, u32[]{:S(2)}, u32[]{:S(2)}) %collective-permute-start.18) | collective-permute-done | bytes 10272 | tf_op jit(solution)/shard_map/ppermute | solution.py:42
  129.4 2.1 %copy.554 = f32[2,128,10,1]{3,2,1,0:T(8,128)} copy(f32[2,128,10,1]{1,0,3,2:T(2,128)S(1)} %collective-permute-done.18) | data formatting | bytes 20480 | tf_op jit(solution)/shard_map/ppermute | solution.py:42
  131.5 5.2 %select_maximum_fusion = f32[2,130,10,130]{3,2,1,0:T(8,128)S(1)} fusion(f32[2,128,10,1]{3,2,1,0:T(8,128)} %copy.554, f32[2,128,10,1]{3,2,1,0:T(8,128)S(1)} %copy.553, f32[2,128,1,128]{3,2,1,0:T(1,128)S(1)} %collective-permute-done.16, f32[2,128,1,128]{3,2,1,0:T(1,128)S(1)} %collective-permute-done.15, f32[1,128,8,128]{3,2,1,0:T(8,128)S(1)} %bitcast.242, ...), kind=kLoop, calls=%fused_computation.3 | loop fusion | flops 4732000 | bytes 2683200 | tf_op jit(solution)/shard_map/concatenate | solution.py:38
  136.7 1.8 %slice_bitcast_fusion.1 = (f32[130,10,130]{2,1,0:T(8,128)S(1)}, f32[130,10,130]{2,1,0:T(8,128)}) fusion(f32[2,130,10,130]{3,2,1,0:T(8,128)S(1)} %select_maximum_fusion), kind=kLoop, calls=%fused_computation.10 | loop fusion | bytes 2704000 | tf_op jit(solution)/shard_map/squeeze | solution.py:89
  138.6 7.8 %fusion.15 = f32[128,8,128]{2,1,0:T(8,128)} fusion(f32[128,8,128]{2,1,0:T(8,128)S(1)} %copy-done.5, f32[130,10,130]{2,1,0:T(8,128)} %get-tuple-element.24, f32[130,10,130]{2,1,0:T(8,128)S(1)} %get-tuple-element.23), kind=kLoop, calls=%fused_computation.33 | loop fusion | flops 3932160 | bytes 8388608 | tf_op jit(solution)/shard_map/add | solution.py:144
  (392 shorter events, 39.5 us)
Async XLA Ops:
  0.6 32.9 %all-to-all-start = ((f32[8,128,128]{2,0,1:T(8,128)}), f32[8,128,128]{2,0,1:T(8,128)S(1)}, u32[]{:S(2)}, u32[]{:S(2)}) async-start(f32[8,128,128]{2,0,1:T(8,128)} %bitcast.239), calls=%async_computation | async-start | bytes 1048576 | tf_op jit(solution)/shard_map/all_to_all | solution.py:116
  11.3 4.4 %collective-permute-start = (f32[8,8,128]{2,1,0:T(8,128)S(1)}, f32[8,8,128]{2,1,0:T(8,128)S(1)}, u32[]{:S(2)}, u32[]{:S(2)}) collective-permute-start(f32[8,8,128]{2,1,0:T(8,128)S(1)} %bitcast.313), channel_id=1, source_target_pairs={{0,2},{2,0},{4,6},{6,4},{8,10},{10,8},{12,14},{14,12},{16,18},{18,... | collective-permute-start | bytes 98312 | tf_op jit(solution)/shard_map/ppermute | solution.py:27
  11.7 4.1 %collective-permute-start.1 = (f32[8,8,128]{2,1,0:T(8,128)S(1)}, f32[8,8,128]{2,1,0:T(8,128)S(1)}, u32[]{:S(2)}, u32[]{:S(2)}) collective-permute-start(f32[8,8,128]{2,1,0:T(8,128)S(1)} %bitcast.312), channel_id=1, source_target_pairs={{0,4},{2,6},{4,0},{6,2},{8,12},{10,14},{12,8},{14,10},{16,20},{18,... | collective-permute-start | bytes 98312 | tf_op jit(solution)/shard_map/ppermute | solution.py:27
  12.0 6.4 %collective-permute-start.2 = (f32[8,8,128]{2,1,0:T(8,128)S(1)}, f32[8,8,128]{2,1,0:T(8,128)S(1)}, u32[]{:S(2)}, u32[]{:S(2)}) collective-permute-start(f32[8,8,128]{2,1,0:T(8,128)S(1)} %bitcast.311), channel_id=1, source_target_pairs={{0,6},{2,4},{4,2},{6,0},{8,14},{10,12},{12,10},{14,8},{16,22},{18,... | collective-permute-start | bytes 98312 | tf_op jit(solution)/shard_map/ppermute | solution.py:27
  13.6 6.9 %collective-permute-start.3 = (f32[8,8,128]{2,1,0:T(8,128)S(1)}, f32[8,8,128]{2,1,0:T(8,128)S(1)}, u32[]{:S(2)}, u32[]{:S(2)}) collective-permute-start(f32[8,8,128]{2,1,0:T(8,128)S(1)} %bitcast.309), channel_id=1, source_target_pairs={{0,8},{2,10},{4,12},{6,14},{8,0},{10,2},{12,4},{14,6},{16,24},{18,... | collective-permute-start | bytes 98312 | tf_op jit(solution)/shard_map/ppermute | solution.py:27
  14.0 7.1 %collective-permute-start.4 = (f32[8,8,128]{2,1,0:T(8,128)S(1)}, f32[8,8,128]{2,1,0:T(8,128)S(1)}, u32[]{:S(2)}, u32[]{:S(2)}) collective-permute-start(f32[8,8,128]{2,1,0:T(8,128)S(1)} %bitcast.308), channel_id=1, source_target_pairs={{0,10},{2,8},{4,14},{6,12},{8,2},{10,0},{12,6},{14,4},{16,26},{18,... | collective-permute-start | bytes 98312 | tf_op jit(solution)/shard_map/ppermute | solution.py:27
  15.7 7.5 %collective-permute-start.5 = (f32[8,8,128]{2,1,0:T(8,128)S(1)}, f32[8,8,128]{2,1,0:T(8,128)S(1)}, u32[]{:S(2)}, u32[]{:S(2)}) collective-permute-start(f32[8,8,128]{2,1,0:T(8,128)S(1)} %bitcast.314), channel_id=1, source_target_pairs={{0,12},{2,14},{4,8},{6,10},{8,4},{10,6},{12,0},{14,2},{16,28},{18,... | collective-permute-start | bytes 98312 | tf_op jit(solution)/shard_map/ppermute | solution.py:27
  15.8 8.9 %collective-permute-start.6 = (f32[8,8,128]{2,1,0:T(8,128)S(1)}, f32[8,8,128]{2,1,0:T(8,128)S(1)}, u32[]{:S(2)}, u32[]{:S(2)}) collective-permute-start(f32[8,8,128]{2,1,0:T(8,128)S(1)} %bitcast.310), channel_id=1, source_target_pairs={{0,14},{2,12},{4,10},{6,8},{8,6},{10,4},{12,2},{14,0},{16,30},{18,... | collective-permute-start | bytes 98312 | tf_op jit(solution)/shard_map/ppermute | solution.py:27
  18.4 7.4 %collective-permute-start.7 = (f32[8,8,128]{2,1,0:T(8,128)S(1)}, f32[8,8,128]{2,1,0:T(8,128)S(1)}, u32[]{:S(2)}, u32[]{:S(2)}) collective-permute-start(f32[8,8,128]{2,1,0:T(8,128)S(1)} %bitcast.307), channel_id=1, source_target_pairs={{0,16},{2,18},{4,20},{6,22},{8,24},{10,26},{12,28},{14,30},{16,0},... | collective-permute-start | bytes 98312 | tf_op jit(solution)/shard_map/ppermute | solution.py:27
  20.5 5.8 %collective-permute-start.8 = (f32[8,8,128]{2,1,0:T(8,128)S(1)}, f32[8,8,128]{2,1,0:T(8,128)S(1)}, u32[]{:S(2)}, u32[]{:S(2)}) collective-permute-start(f32[8,8,128]{2,1,0:T(8,128)S(1)} %bitcast.306), channel_id=1, source_target_pairs={{0,18},{2,16},{4,22},{6,20},{8,26},{10,24},{12,30},{14,28},{16,2},... | collective-permute-start | bytes 98312 | tf_op jit(solution)/shard_map/ppermute | solution.py:27
  21.0 6.5 %collective-permute-start.9 = (f32[8,8,128]{2,1,0:T(8,128)S(1)}, f32[8,8,128]{2,1,0:T(8,128)S(1)}, u32[]{:S(2)}, u32[]{:S(2)}) collective-permute-start(f32[8,8,128]{2,1,0:T(8,128)S(1)} %bitcast.305), channel_id=1, source_target_pairs={{0,20},{2,22},{4,16},{6,18},{8,28},{10,30},{12,24},{14,26},{16,4},... | collective-permute-start | bytes 98312 | tf_op jit(solution)/shard_map/ppermute | solution.py:27
  23.1 5.9 %collective-permute-start.10 = (f32[8,8,128]{2,1,0:T(8,128)S(1)}, f32[8,8,128]{2,1,0:T(8,128)S(1)}, u32[]{:S(2)}, u32[]{:S(2)}) collective-permute-start(f32[8,8,128]{2,1,0:T(8,128)S(1)} %bitcast.304), channel_id=1, source_target_pairs={{0,22},{2,20},{4,18},{6,16},{8,30},{10,28},{12,26},{14,24},{16,6},... | collective-permute-start | bytes 98312 | tf_op jit(solution)/shard_map/ppermute | solution.py:27
  24.7 4.6 %collective-permute-start.11 = (f32[8,8,128]{2,1,0:T(8,128)S(1)}, f32[8,8,128]{2,1,0:T(8,128)S(1)}, u32[]{:S(2)}, u32[]{:S(2)}) collective-permute-start(f32[8,8,128]{2,1,0:T(8,128)S(1)} %bitcast.303), channel_id=1, source_target_pairs={{0,24},{2,26},{4,28},{6,30},{8,16},{10,18},{12,20},{14,22},{16,8},... | collective-permute-start | bytes 98312 | tf_op jit(solution)/shard_map/ppermute | solution.py:27
  25.8 4.7 %collective-permute-start.12 = (f32[8,8,128]{2,1,0:T(8,128)S(1)}, f32[8,8,128]{2,1,0:T(8,128)S(1)}, u32[]{:S(2)}, u32[]{:S(2)}) collective-permute-start(f32[8,8,128]{2,1,0:T(8,128)S(1)} %bitcast.302), channel_id=1, source_target_pairs={{0,26},{2,24},{4,30},{6,28},{8,18},{10,16},{12,22},{14,20},{16,10}... | collective-permute-start | bytes 98312 | tf_op jit(solution)/shard_map/ppermute | solution.py:27
  26.4 4.7 %collective-permute-start.13 = (f32[8,8,128]{2,1,0:T(8,128)S(1)}, f32[8,8,128]{2,1,0:T(8,128)S(1)}, u32[]{:S(2)}, u32[]{:S(2)}) collective-permute-start(f32[8,8,128]{2,1,0:T(8,128)S(1)} %bitcast.301), channel_id=1, source_target_pairs={{0,28},{2,30},{4,24},{6,26},{8,20},{10,22},{12,16},{14,18},{16,12}... | collective-permute-start | bytes 98312 | tf_op jit(solution)/shard_map/ppermute | solution.py:27
  27.6 5.3 %collective-permute-start.14 = (f32[8,8,128]{2,1,0:T(8,128)S(1)}, f32[8,8,128]{2,1,0:T(8,128)S(1)}, u32[]{:S(2)}, u32[]{:S(2)}) collective-permute-start(f32[8,8,128]{2,1,0:T(8,128)S(1)} %bitcast.300), channel_id=1, source_target_pairs={{0,30},{2,28},{4,26},{6,24},{8,22},{10,20},{12,18},{14,16},{16,14}... | collective-permute-start | bytes 98312 | tf_op jit(solution)/shard_map/ppermute | solution.py:27
  34.4 11.2 %all-to-all-start.2 = ((f32[128,8,128]{2,1,0:T(8,128)}), f32[128,8,128]{2,1,0:T(8,128)S(1)}, u32[]{:S(2)}, u32[]{:S(2)}) async-start(f32[128,8,128]{2,1,0:T(8,128)} %bitcast.59), calls=%async_computation.2 | async-start | bytes 1048576 | tf_op jit(solution)/shard_map/all_to_all | solution.py:127
  45.6 10.3 %all-to-all-start.1 = ((f32[128,8,128]{2,1,0:T(8,128)}), f32[128,8,128]{2,1,0:T(8,128)S(1)}, u32[]{:S(2)}, u32[]{:S(2)}) async-start(f32[128,8,128]{2,1,0:T(8,128)} %bitcast.81), calls=%async_computation.1 | async-start | bytes 1048576 | tf_op jit(solution)/shard_map/all_to_all | solution.py:126
  79.4 27.0 %copy-start.4 = (f32[128,8,128]{2,1,0:T(8,128)S(1)}, f32[128,8,128]{2,1,0:T(8,128)}, u32[]{:S(2)}) copy-start(f32[128,8,128]{2,1,0:T(8,128)} %param.4) | copy-start | bytes 1572868
  79.8 26.9 %copy-start = (f32[128,8,128]{2,1,0:T(8,128)S(1)}, f32[128,8,128]{2,1,0:T(8,128)}, u32[]{:S(2)}) copy-start(f32[128,8,128]{2,1,0:T(8,128)} %param.5) | copy-start | bytes 1572868
  106.9 5.8 %collective-permute-start.15 = (f32[2,128,1,128]{3,2,1,0:T(1,128)S(1)}, f32[2,128,1,128]{3,2,1,0:T(1,128)S(1)}, u32[]{:S(2)}, u32[]{:S(2)}) collective-permute-start(f32[2,128,1,128]{3,2,1,0:T(1,128)S(1)} %get-tuple-element.31), channel_id=1, source_target_pairs={{0,2},{2,4},{4,6},{6,8},{8,10},{10,12},{12,14},{14,16},{16,18},{18... | collective-permute-start | bytes 393224 | tf_op jit(solution)/shard_map/ppermute | solution.py:40
  110.5 7.2 %collective-permute-start.16 = (f32[2,128,1,128]{3,2,1,0:T(1,128)S(1)}, f32[2,128,1,128]{3,2,1,0:T(1,128)S(1)}, u32[]{:S(2)}, u32[]{:S(2)}) collective-permute-start(f32[2,128,1,128]{3,2,1,0:T(1,128)S(1)} %get-tuple-element.32), channel_id=1, source_target_pairs={{2,0},{4,2},{6,4},{8,6},{10,8},{12,10},{14,12},{16,14},{18,16},{20... | collective-permute-start | bytes 393224 | tf_op jit(solution)/shard_map/ppermute | solution.py:42
  122.3 3.9 %collective-permute-start.17 = (f32[2,128,10,1]{1,0,3,2:T(2,128)S(1)}, f32[2,128,10,1]{1,0,3,2:T(2,128)S(1)}, u32[]{:S(2)}, u32[]{:S(2)}) collective-permute-start(f32[2,128,10,1]{1,0,3,2:T(2,128)S(1)} %copy.551), channel_id=1, source_target_pairs={{0,1},{2,3},{4,5},{6,7},{8,9},{10,11},{12,13},{14,15},{16,17},{18,... | collective-permute-start | bytes 30728 | tf_op jit(solution)/shard_map/ppermute | solution.py:40
  125.0 4.4 %collective-permute-start.18 = (f32[2,128,10,1]{1,0,3,2:T(2,128)S(1)}, f32[2,128,10,1]{1,0,3,2:T(2,128)S(1)}, u32[]{:S(2)}, u32[]{:S(2)}) collective-permute-start(f32[2,128,10,1]{1,0,3,2:T(2,128)S(1)} %copy.552), channel_id=1, source_target_pairs={{1,0},{3,2},{5,4},{7,6},{9,8},{11,10},{13,12},{15,14},{17,16},{19,... | collective-permute-start | bytes 30728 | tf_op jit(solution)/shard_map/ppermute | solution.py:42
  (6 other events, 43.8 us)
